TPU v7x, 32 devices: a whole 2x2x4 slice. The times are simulated.
32 devices in a mesh: groups: 2 (over y), chan: 4 (over z), tm: 2 (over x), src: 2 (over core).
Axes of the slice: x: 2, y: 2, z: 4, core: 2. Of those that a mesh axis runs over, the one named last changes fastest.
Arguments:
- raw_records: bfloat16 [8, 4352, 512], P(('groups', 'tm', 'src'), 'chan'), parts along dimension 0, may hold values from -6 to 6
- filter_taps: float32 [64], replicated, may hold values from -0.75 to 0.75
- good_channels: int32 [1024], P(('groups', 'chan')), parts along dimension 0, may hold values 0 or 1
- source_ids: int32 [8, 4], P('groups'), parts along dimension 0, may hold values from 0 to 511
- window_offsets: int32 [8], P(('groups', 'tm', 'src')), parts along dimension 0, may hold values from 0 to 192, as said below
Outputs:
- correlations: float32 [32, 384, 512], P(('groups', 'tm', 'src'), None, 'chan'), parts along dimension 0
There are 2 independent parts, one for each index of `groups`. A program takes and returns all parts, laid end to end along the dimension named above; an argument that names none is the same for every part. Nothing has to cross between parts.
Inputs may be any that keep to these rules, and one draw needn't show every extreme that they name: `window_offsets`: multiples of 4; in every part some window has offset 192.
All inputs are finite; a program needn't handle non-finite values. No bound on the sum of `good_channels` on one device may be relied on, other than what follows from the above.
Results may differ from a plain program's by a relative error of at most 0.0064.
Values may be sent and summed in bfloat16 or wider, within the bound.
A program may use at most 64 MiB of HBM per device.

v0:
```python
import functools
import math

import jax
import jax.numpy as jnp
import ml_dtypes
import numpy as np
from jax import lax
from jax.experimental import pallas as pl
from jax.experimental.pallas import tpu as pltpu
from jax.sharding import PartitionSpec as P

W = 1024
F = 512
TAPS = 64
BANDS = 8
LAGS = 384
MAX_SHIFT = 48
NSRC = 16
LANES = 128
VMEM_LIMIT = 44 * 1024 * 1024
NT = (((1,), (1,)), ((), ()))


def up(value, step):
    return -(-value // step) * step


def layout(samples):
    count = samples // 4
    reach = TAPS // 4 - 1 + MAX_SHIFT
    used = up(count + reach, 16)
    rows = up(used, LANES)
    if used + rows // LANES * NSRC > rows:
        rows = up(used + rows // LANES * NSRC, LANES)
    return count, reach, used, rows


def waves(phase):
    angle = (phase % W).astype(np.float64) * (2.0 * math.pi / W)
    return np.concatenate([np.cos(angle), -np.sin(angle)], axis=0)


def forward_blocks(chans, samples):
    count, reach, used, rows = layout(samples)
    freq = np.arange(1, F + 1, dtype=np.int64)[:, None]
    parts = []
    for owner in range(chans):
        row = np.arange(rows, dtype=np.int64)
        sample = count * owner - reach + row
        inside = (sample >= 0) & (sample < W) & (row < used)
        parts.append(waves(freq * sample[None, :]) * inside[None, :])
    return np.concatenate(parts, axis=1).astype(np.float32).astype(ml_dtypes.bfloat16)


def inverse_rows():
    freq = np.arange(1, F + 1, dtype=np.int64)[:, None]
    shift = np.arange(LAGS, dtype=np.int64)[None, :] - LAGS // 2
    table = waves(freq * shift).astype(np.float32).T
    high = table.astype(ml_dtypes.bfloat16)
    low = (table - high.astype(np.float32)).astype(ml_dtypes.bfloat16)
    return np.ascontiguousarray(high), np.ascontiguousarray(low)


def gather_kernel(sizes, offset, taps, ids, keep, raw, out, toep, blocks, own_sem, send_sem, recv_sem):
    chans, tms, cores = sizes
    samples, channels = raw.shape
    count, reach, used, rows = layout(samples)
    here, tm, core = (lax.axis_index(name) for name in ("chan", "tm", "src"))
    window = tm * cores + core

    barrier = pltpu.get_barrier_semaphore()
    for axis, place, size in (("chan", here, chans), ("tm", tm, tms), ("src", core, cores)):
        for step in range(1, size):
            pl.semaphore_signal(
                barrier,
                inc=1,
                device_id={axis: lax.rem(place + step, size)},
                device_id_type=pl.DeviceIdType.MESH,
            )

    toep[...] = jnp.zeros_like(toep)
    row = lax.broadcasted_iota(jnp.int32, (32, 384), 0)
    col = lax.broadcasted_iota(jnp.int32, (32, 384), 1)
    tap_group = (col >> 2) - row - 1 - (offset[0] >> 2)
    base = jnp.zeros((32, 384), jnp.float32)
    for group in range(TAPS // 4):
        base = jnp.where(tap_group == group, taps[group : group + 1, :], base)
    high = base.astype(jnp.bfloat16)
    low = (base - high.astype(jnp.float32)).astype(jnp.bfloat16)
    for block in range(rows // 32):
        span = slice(128 * block, 128 * block + 384)
        toep[0, 32 * block : 32 * block + 32, span] = high
        toep[1, 32 * block : 32 * block + 32, span] = low
    lead = 4 * (reach + 1)
    samples_in = raw[...]
    total = jnp.dot(toep[0, :, lead : lead + samples], samples_in, preferred_element_type=jnp.float32)
    total += jnp.dot(toep[1, :, lead : lead + samples], samples_in, preferred_element_type=jnp.float32)
    filtered = total.astype(jnp.bfloat16)
    channel = lax.broadcasted_iota(jnp.int32, (NSRC, channels), 1)
    pick = jnp.where(channel == ids[...], 1.0, 0.0).astype(jnp.bfloat16)
    picked = lax.dot_general(pick, filtered, NT, preferred_element_type=jnp.float32).astype(jnp.bfloat16)
    keep_rows = jnp.broadcast_to(keep[...], (16, LANES)).astype(jnp.bfloat16)
    for owner in range(chans):
        blocks[owner, :used, :] = filtered[:used, owner * LANES : (owner + 1) * LANES]
        for tile in range((rows - used) // NSRC):
            at = used + tile * NSRC
            lanes = slice(tile * LANES, (tile + 1) * LANES)
            if tile < rows // LANES:
                blocks[owner, at : at + NSRC, :] = picked[:, lanes]
            else:
                blocks[owner, at : at + NSRC, :] = jnp.zeros((NSRC, LANES), jnp.bfloat16)
        blocks[owner, rows:, :] = keep_rows

    pl.semaphore_wait(barrier, chans + tms + cores - 3)

    sent = []

    def slot(part, owner):
        return out.at[part, owner]

    def send(source, part, owner, target):
        copy = pltpu.make_async_remote_copy(
            src_ref=source,
            dst_ref=slot(part, owner),
            send_sem=send_sem.at[len(sent)],
            recv_sem=recv_sem.at[part * chans + owner],
            device_id=target,
            device_id_type=pl.DeviceIdType.MESH,
        )
        copy.start()
        sent.append(copy)

    def arrive(part, owner):
        pltpu.make_async_remote_copy(
            src_ref=slot(part, owner),
            dst_ref=slot(part, owner),
            send_sem=send_sem.at[0],
            recv_sem=recv_sem.at[part * chans + owner],
            device_id={"chan": here},
            device_id_type=pl.DeviceIdType.MESH,
        ).wait_recv()

    def to_cores(part, owner):
        for step in range(1, cores):
            send(slot(part, owner), part, owner, {"src": lax.rem(core + step, cores)})

    for step in range(1, chans):
        there = lax.rem(here + step, chans)
        send(blocks.at[there], window, here, {"chan": there})
    own = pltpu.make_async_copy(blocks.at[here], slot(window, here), own_sem)
    own.start()
    own.wait()
    for step in range(chans):
        owner = lax.rem(here + chans - step, chans)
        if step:
            arrive(window, owner)
        for hop in range(1, tms):
            send(slot(window, owner), window, owner, {"tm": lax.rem(tm + hop, tms)})
        to_cores(window, owner)
    for step in range(chans):
        owner = lax.rem(here + chans - step, chans)
        for hop in range(1, tms):
            part = lax.rem(tm + tms - hop, tms) * cores + core
            arrive(part, owner)
            to_cores(part, owner)
    for step in range(chans):
        owner = lax.rem(here + chans - step, chans)
        for hop in range(tms):
            for turn in range(1, cores):
                part = lax.rem(tm + tms - hop, tms) * cores + lax.rem(core + turn, cores)
                arrive(part, owner)
    for copy in sent:
        copy.wait_send()


def correlate_kernel(sizes, samples, ids, keep, table, inv_high, inv_low, blocks, out, spec, src_spec, cross):
    chans, tms, cores = sizes
    windows = tms * cores
    _, _, used, rows = layout(samples)
    mine = NSRC // windows
    window = lax.axis_index("tm") * cores + lax.axis_index("src")
    width = 2 if windows % 2 == 0 else 1
    for first in range(0, windows, width):
        data = jnp.concatenate(
            [
                jnp.concatenate([blocks[part, owner, :rows, :] for owner in range(chans)], axis=0)
                for part in range(first, first + width)
            ],
            axis=1,
        )
        spec[:, first * LANES : (first + width) * LANES] = jnp.dot(
            table[...], data, preferred_element_type=jnp.float32
        )
    tiles = rows // LANES
    series = jnp.concatenate(
        [
            jnp.concatenate(
                [
                    blocks[part, owner, used + NSRC * tile : used + NSRC * (tile + 1), :]
                    for owner in range(chans)
                    for tile in range(tiles)
                ],
                axis=1,
            )
            for part in range(windows)
        ],
        axis=0,
    )
    src_spec[...] = lax.dot_general(table[...], series, NT, preferred_element_type=jnp.float32)

    channel = lax.broadcasted_iota(jnp.int32, (NSRC, LANES), 1)
    src_keep = jnp.zeros((NSRC, 1), jnp.float32)
    for owner in range(chans):
        flags = blocks[0, owner, rows : rows + 16, :].astype(jnp.float32)
        hit = channel + owner * LANES == ids[...]
        src_keep += jnp.sum(jnp.where(hit, flags, 0.0), axis=1, keepdims=True)
    number = lax.broadcasted_iota(jnp.int32, (NSRC, mine * LANES), 0)
    wanted = lax.broadcasted_iota(jnp.int32, (NSRC, mine * LANES), 1) // LANES + window * mine
    spread = (jnp.where(number == wanted, 1.0, 0.0) * src_keep).astype(jnp.bfloat16)
    keep_lanes = jnp.concatenate([keep[...]] * windows, axis=1)
    size = F // BANDS

    def whiten(real, imag, gain):
        power = jnp.mean(real * real + imag * imag, axis=0, keepdims=True)
        factor = gain / jnp.sqrt(power + 1e-06)
        return (real * factor).astype(jnp.bfloat16), (imag * factor).astype(jnp.bfloat16)

    @pl.loop(0, BANDS)
    def _(band):
        at_real = pl.ds(pl.multiple_of(band * size, size), size)
        at_imag = pl.ds(pl.multiple_of(F + band * size, size), size)
        real, imag = whiten(spec[at_real, :], spec[at_imag, :], keep_lanes)
        real, imag = real.astype(jnp.float32), imag.astype(jnp.float32)
        src = jnp.concatenate(
            whiten(src_spec[at_real, :], src_spec[at_imag, :], 1.0), axis=0
        )
        cross_real = [0.0] * mine
        cross_imag = [0.0] * mine
        for part in range(windows):
            wide = jnp.dot(
                src[:, part * NSRC : (part + 1) * NSRC], spread, preferred_element_type=jnp.float32
            )
            xr = real[:, part * LANES : (part + 1) * LANES]
            xi = imag[:, part * LANES : (part + 1) * LANES]
            for one in range(mine):
                sr = wide[:size, one * LANES : (one + 1) * LANES]
                si = wide[size:, one * LANES : (one + 1) * LANES]
                cross_real[one] = cross_real[one] + (sr * xr + si * xi)
                cross_imag[one] = cross_imag[one] + (sr * xi - si * xr)
        for one in range(mine):
            lanes = slice(one * LANES, (one + 1) * LANES)
            for at, value in ((at_real, cross_real[one]), (at_imag, cross_imag[one])):
                high = value.astype(jnp.bfloat16)
                cross[0, at, lanes] = high
                cross[1, at, lanes] = (value - high.astype(jnp.float32)).astype(jnp.bfloat16)

    scale = 1.0 / math.sqrt(windows * F)
    total = jnp.dot(inv_high[...], cross[0], preferred_element_type=jnp.float32)
    total += jnp.dot(inv_high[...], cross[1], preferred_element_type=jnp.float32)
    total += jnp.dot(inv_low[...], cross[0], preferred_element_type=jnp.float32)
    for one in range(mine):
        out[one] = total[:, one * LANES : (one + 1) * LANES] * scale


def body(sizes, table, inv_high, inv_low, raw_records, filter_taps, good_channels, source_ids, window_offsets):
    chans, tms, cores = sizes
    windows = tms * cores
    samples, channels = raw_records.shape[1:]
    count, reach, used, rows = layout(samples)
    ids = source_ids.reshape(NSRC, 1)
    keep = good_channels.astype(jnp.float32).reshape(1, LANES)
    taps = jnp.tile(filter_taps.reshape(TAPS // 4, 4), (1, 96))
    vmem = pl.BlockSpec(memory_space=pltpu.VMEM)
    smem = pl.BlockSpec(memory_space=pltpu.SMEM)
    copies = chans - 1 + chans * (tms - 1 + cores - 1 + (tms - 1) * (cores - 1))
    gathered = pl.pallas_call(
        functools.partial(gather_kernel, sizes),
        out_shape=jax.ShapeDtypeStruct((windows, chans, rows + 16, LANES), jnp.bfloat16),
        in_specs=[smem, vmem, vmem, vmem, vmem],
        out_specs=vmem,
        scratch_shapes=[
            pltpu.VMEM((2, rows, 4 * rows + 256), jnp.bfloat16),
            pltpu.VMEM((chans, rows + 16, LANES), jnp.bfloat16),
            pltpu.SemaphoreType.DMA,
            pltpu.SemaphoreType.DMA((copies,)),
            pltpu.SemaphoreType.DMA((windows * chans,)),
        ],
        compiler_params=pltpu.CompilerParams(
            collective_id=0, has_side_effects=True, vmem_limit_bytes=VMEM_LIMIT
        ),
        name="gather",
    )(window_offsets, taps, ids, keep, raw_records.reshape(samples, channels))
    mine = NSRC // windows
    return pl.pallas_call(
        functools.partial(correlate_kernel, sizes, samples),
        out_shape=jax.ShapeDtypeStruct((mine, LAGS, LANES), jnp.float32),
        in_specs=[vmem] * 6,
        out_specs=vmem,
        scratch_shapes=[
            pltpu.VMEM((2 * F, windows * LANES), jnp.float32),
            pltpu.VMEM((2 * F, windows * NSRC), jnp.float32),
            pltpu.VMEM((2, 2 * F, mine * LANES), jnp.bfloat16),
        ],
        compiler_params=pltpu.CompilerParams(vmem_limit_bytes=VMEM_LIMIT),
        name="correlate",
    )(ids, keep, table, inv_high, inv_low, gathered)


def solution(mesh):
    placed = (
        P(("groups", "tm", "src"), "chan", None),
        P(),
        P(("groups", "chan")),
        P("groups", None),
        P(("groups", "tm", "src")),
    )
    sizes = tuple(mesh.shape[name] for name in ("chan", "tm", "src"))

    def run(raw_records, *rest):
        table = forward_blocks(sizes[0], raw_records.shape[1])
        inv_high, inv_low = inverse_rows()
        return body(sizes, table, inv_high, inv_low, raw_records, *rest)

    def call(raw_records, *rest):
        return jax.shard_map(
            run,
            mesh=mesh,
            in_specs=placed,
            out_specs=P(("groups", "tm", "src"), None, "chan"),
            check_vma=False,
        )(raw_records, *rest)

    return call
```

profile of v0, /device:TPU:0, one launch (start us, length us, event | category | flops | bytes accessed | tf_op | source)
XLA Modules:
  0.0 35.5 jit_solution(4684724841108650841)
XLA Ops:
  0.0 0.0 copy-start
  0.8 0.8 %convert_bitcast_fusion.keep = f32[1,128]{1,0:T(1,128)S(1)} fusion(s32[128]{0:T(128)} %param.10), kind=kLoop, calls=%fused_computation | loop fusion | flops 128 | bytes 1024 | tf_op jit(solution)/shard_map/reshape | solution.py:272
  1.6 0.8 %reshape.16.ids = s32[16,1]{1,0:T(8,128)S(1)} reshape(s32[4,4]{1,0:T(4,128)} %param.11) | data formatting | bytes 128 | tf_op jit(solution)/shard_map/reshape | solution.py:271
  2.4 0.7 %tile.10 = f32[16,4]{1,0:T(8,128)S(1)} reshape(f32[64]{0:T(128)} %param.9) | data formatting | bytes 512 | tf_op jit(solution)/shard_map/tile | solution.py:273
  3.1 0.1 copy.11
  3.2 0.1 copy.12.taps
  3.3 0.0 copy-start.1
  3.3 1.3 %copy-done.1 = bf16[1,1088,512]{2,1,0:T(8,128)(2,1)S(1)} copy-done((bf16[1,1088,512]{2,1,0:T(8,128)(2,1)S(1)}, bf16[1,1088,512]{2,1,0:T(8,128)(2,1)}, u32[]{:S(2)}) %copy-start.1) | copy-done | bytes 1114136
  4.6 20.2 %gather.1.blocks = bf16[4,4,400,128]{3,2,1,0:T(8,128)(2,1)S(1)} custom-call(s32[1]{0:T(128)S(6)} %copy.15.offset, f32[16,384]{1,0:T(8,128)S(1)} %copy.12.taps, s32[16,1]{1,0:T(8,128)S(1)} %reshape.16.ids, f32[1,128]{1,0:T(1,128)S(1)} %convert_bitcast_fusion.keep, bf16[1088,512]{1,0:T(8,128)(2,1)S(1)} %bitcast.4), custom_call_target="tpu_custom_call" | custom-call | tf_op jit(solution)/shard_map/gather/pallas_call | solution.py:277
  24.8 0.0 copy-done
  24.8 0.0 copy-start.2
  24.8 1.1 %copy-done.2 = bf16[384,1024]{1,0:T(8,128)(2,1)S(1)} copy-done((bf16[384,1024]{1,0:T(8,128)(2,1)S(1)}, bf16[384,1024]{1,0:T(8,128)(2,1)}, u32[]{:S(2)}) %copy-start.2) | copy-done | bytes 786456
  25.9 0.0 copy-start.3
  25.9 1.1 %copy-done.3 = bf16[384,1024]{1,0:T(8,128)(2,1)S(1)} copy-done((bf16[384,1024]{1,0:T(8,128)(2,1)S(1)}, bf16[384,1024]{1,0:T(8,128)(2,1)}, u32[]{:S(2)}) %copy-start.3) | copy-done | bytes 786456
  27.1 8.4 %correlate.1 = f32[4,384,128]{2,1,0:T(8,128)} custom-call(s32[16,1]{1,0:T(8,128)S(1)} %reshape.16.ids, f32[1,128]{1,0:T(1,128)S(1)} %convert_bitcast_fusion.keep, bf16[1024,1536]{1,0:T(8,128)(2,1)S(1)} %copy-done, bf16[384,1024]{1,0:T(8,128)(2,1)S(1)} %copy-done.3, bf16[384,1024]{1,0:T(8,128)(2,1)S(1)} %copy-done.2, bf16[4,4,400,128]{3,2,1,0:T(8,128)(2,1)S(1)} %gather.1.blocks), custom_call_target="tpu_custom_call" | custom-call | tf_op jit(solution)/shard_map/correlate/pallas_call | solution.py:295
  (1 shorter events, 0.0 us)
Async XLA Ops:
  0.0 24.8 %copy-start = (bf16[1024,1536]{1,0:T(8,128)(2,1)S(1)}, bf16[1024,1536]{1,0:T(8,128)(2,1)}, u32[]{:S(2)}) copy-start(bf16[1024,1536]{1,0:T(8,128)(2,1)} %constant.6.clone.table) | copy-start | bytes 9437188
  3.3 1.3 %copy-start.1 = (bf16[1,1088,512]{2,1,0:T(8,128)(2,1)S(1)}, bf16[1,1088,512]{2,1,0:T(8,128)(2,1)}, u32[]{:S(2)}) copy-start(bf16[1,1088,512]{2,1,0:T(8,128)(2,1)} %param.8) | copy-start | bytes 3342340
  24.8 1.1 %copy-start.2 = (bf16[384,1024]{1,0:T(8,128)(2,1)S(1)}, bf16[384,1024]{1,0:T(8,128)(2,1)}, u32[]{:S(2)}) copy-start(bf16[384,1024]{1,0:T(8,128)(2,1)} %constant.8.clone.inv_low) | copy-start | bytes 2359300
  25.9 1.1 %copy-start.3 = (bf16[384,1024]{1,0:T(8,128)(2,1)S(1)}, bf16[384,1024]{1,0:T(8,128)(2,1)}, u32[]{:S(2)}) copy-start(bf16[384,1024]{1,0:T(8,128)(2,1)} %constant.7.clone.inv_high) | copy-start | bytes 2359300
where the time goes:
time: 35.8 us; the launch traced here: 35.5 us
  Pallas kernels  28.6 us (80%)
  local copies, waits for them, and re-layouts  5.23 us (15%)
  between operations  0.84 us (2%)
  other arithmetic  0.81 us (2%)
    pallas_call x1, Pallas kernels, body(): pl.pallas_call(functools.partial(gather_kernel, sizes), out_shape=jax.Sha...  20.2 us
    pallas_call x1, Pallas kernels, body(): pl.pallas_call(functools.partial(correlate_kernel, sizes, samples), out_s...  8.45 us
    unnamed x8, local copies, waits for them, and re-layouts  3.54 us
    another operation x4, local copies, waits for them, and re-layouts, body(): taps = jnp.tile(filter_taps.reshape(TAPS // 4, 4), (1, 96))  0.94 us
    reshape x1, other arithmetic, body(): keep = good_channels.astype(jnp.float32).reshape(1, LANES)  0.81 us
    reshape x1, local copies, waits for them, and re-layouts, body(): ids = source_ids.reshape(NSRC, 1)  0.76 us

commit v1 on v0

--- a/solution.py
+++ b/solution.py
@@ -18,7 +18,8 @@
 MAX_SHIFT = 48
 NSRC = 16
 LANES = 128
-VMEM_LIMIT = 44 * 1024 * 1024
+GATHER_VMEM = 24 * 1024 * 1024
+CORRELATE_VMEM = 48 * 1024 * 1024
 NT = (((1,), (1,)), ((), ()))
 
 
@@ -62,7 +63,20 @@
     return np.ascontiguousarray(high), np.ascontiguousarray(low)
 
 
-def gather_kernel(sizes, offset, taps, ids, keep, raw, out, toep, blocks, own_sem, send_sem, recv_sem):
+def id_column(ids):
+    number = lax.broadcasted_iota(jnp.int32, (NSRC, 1), 0)
+    column = jnp.zeros((NSRC, 1), jnp.int32)
+    per_step = ids.shape[1]
+    for source in range(NSRC):
+        column = jnp.where(number == source, ids[source // per_step, source % per_step], column)
+    return column
+
+
+def gather_kernel(
+    sizes, offset, taps, ids, keep, raw_hbm, out, raw, toep, blocks, raw_sem, own_sem, send_sem, recv_sem
+):
+    read = pltpu.make_async_copy(raw_hbm, raw, raw_sem)
+    read.start()
     chans, tms, cores = sizes
     samples, channels = raw.shape
     count, reach, used, rows = layout(samples)
@@ -82,10 +96,10 @@
     toep[...] = jnp.zeros_like(toep)
     row = lax.broadcasted_iota(jnp.int32, (32, 384), 0)
     col = lax.broadcasted_iota(jnp.int32, (32, 384), 1)
-    tap_group = (col >> 2) - row - 1 - (offset[0] >> 2)
+    tap_at = col - 4 * row - 4 - offset[0]
     base = jnp.zeros((32, 384), jnp.float32)
-    for group in range(TAPS // 4):
-        base = jnp.where(tap_group == group, taps[group : group + 1, :], base)
+    for tap in range(TAPS):
+        base = jnp.where(tap_at == tap, taps[tap], base)
     high = base.astype(jnp.bfloat16)
     low = (base - high.astype(jnp.float32)).astype(jnp.bfloat16)
     for block in range(rows // 32):
@@ -93,14 +107,15 @@
         toep[0, 32 * block : 32 * block + 32, span] = high
         toep[1, 32 * block : 32 * block + 32, span] = low
     lead = 4 * (reach + 1)
+    read.wait()
     samples_in = raw[...]
     total = jnp.dot(toep[0, :, lead : lead + samples], samples_in, preferred_element_type=jnp.float32)
     total += jnp.dot(toep[1, :, lead : lead + samples], samples_in, preferred_element_type=jnp.float32)
     filtered = total.astype(jnp.bfloat16)
     channel = lax.broadcasted_iota(jnp.int32, (NSRC, channels), 1)
-    pick = jnp.where(channel == ids[...], 1.0, 0.0).astype(jnp.bfloat16)
+    pick = jnp.where(channel == id_column(ids), 1.0, 0.0).astype(jnp.bfloat16)
     picked = lax.dot_general(pick, filtered, NT, preferred_element_type=jnp.float32).astype(jnp.bfloat16)
-    keep_rows = jnp.broadcast_to(keep[...], (16, LANES)).astype(jnp.bfloat16)
+    keep_rows = jnp.broadcast_to(keep[...].astype(jnp.float32), (16, LANES)).astype(jnp.bfloat16)
     for owner in range(chans):
         blocks[owner, :used, :] = filtered[:used, owner * LANES : (owner + 1) * LANES]
         for tile in range((rows - used) // NSRC):
@@ -150,14 +165,16 @@
         send(blocks.at[there], window, here, {"chan": there})
     own = pltpu.make_async_copy(blocks.at[here], slot(window, here), own_sem)
     own.start()
-    own.wait()
     for step in range(chans):
         owner = lax.rem(here + chans - step, chans)
         if step:
             arrive(window, owner)
+        source = slot(window, owner) if step else blocks.at[here]
         for hop in range(1, tms):
-            send(slot(window, owner), window, owner, {"tm": lax.rem(tm + hop, tms)})
-        to_cores(window, owner)
+            send(source, window, owner, {"tm": lax.rem(tm + hop, tms)})
+        for turn in range(1, cores):
+            send(source, window, owner, {"src": lax.rem(core + turn, cores)})
+    own.wait()
     for step in range(chans):
         owner = lax.rem(here + chans - step, chans)
         for hop in range(1, tms):
@@ -174,24 +191,38 @@
         copy.wait_send()
 
 
-def correlate_kernel(sizes, samples, ids, keep, table, inv_high, inv_low, blocks, out, spec, src_spec, cross):
+def correlate_kernel(
+    sizes, samples, ids, keep, table_hbm, high_hbm, low_hbm, blocks, out, spec, src_spec, cross, tables, inv_high, inv_low, sems
+):
+    quarter = F // 2
+    table_reads = [
+        pltpu.make_async_copy(table_hbm.at[pl.ds(part * quarter, quarter)], tables.at[part], sems.at[2 + part])
+        for part in range(4)
+    ]
+    for read in table_reads:
+        read.start()
+    reads = [
+        pltpu.make_async_copy(high_hbm, inv_high, sems.at[0]),
+        pltpu.make_async_copy(low_hbm, inv_low, sems.at[1]),
+    ]
+    for read in reads:
+        read.start()
     chans, tms, cores = sizes
     windows = tms * cores
     _, _, used, rows = layout(samples)
     mine = NSRC // windows
     window = lax.axis_index("tm") * cores + lax.axis_index("src")
     width = 2 if windows % 2 == 0 else 1
-    for first in range(0, windows, width):
-        data = jnp.concatenate(
+    pairs = [
+        jnp.concatenate(
             [
                 jnp.concatenate([blocks[part, owner, :rows, :] for owner in range(chans)], axis=0)
                 for part in range(first, first + width)
             ],
             axis=1,
         )
-        spec[:, first * LANES : (first + width) * LANES] = jnp.dot(
-            table[...], data, preferred_element_type=jnp.float32
-        )
+        for first in range(0, windows, width)
+    ]
     tiles = rows // LANES
     series = jnp.concatenate(
         [
@@ -207,18 +238,26 @@
         ],
         axis=0,
     )
-    src_spec[...] = lax.dot_general(table[...], series, NT, preferred_element_type=jnp.float32)
+    for number, read in enumerate(table_reads):
+        read.wait()
+        table = tables[number]
+        at = slice(number * quarter, (number + 1) * quarter)
+        for pair, data in enumerate(pairs):
+            lanes = slice(pair * width * LANES, (pair + 1) * width * LANES)
+            spec[at, lanes] = jnp.dot(table, data, preferred_element_type=jnp.float32)
+        src_spec[at, :] = lax.dot_general(table, series, NT, preferred_element_type=jnp.float32)
 
     channel = lax.broadcasted_iota(jnp.int32, (NSRC, LANES), 1)
+    id_at = id_column(ids)
     src_keep = jnp.zeros((NSRC, 1), jnp.float32)
     for owner in range(chans):
         flags = blocks[0, owner, rows : rows + 16, :].astype(jnp.float32)
-        hit = channel + owner * LANES == ids[...]
+        hit = channel + owner * LANES == id_at
         src_keep += jnp.sum(jnp.where(hit, flags, 0.0), axis=1, keepdims=True)
     number = lax.broadcasted_iota(jnp.int32, (NSRC, mine * LANES), 0)
     wanted = lax.broadcasted_iota(jnp.int32, (NSRC, mine * LANES), 1) // LANES + window * mine
     spread = (jnp.where(number == wanted, 1.0, 0.0) * src_keep).astype(jnp.bfloat16)
-    keep_lanes = jnp.concatenate([keep[...]] * windows, axis=1)
+    keep_lanes = jnp.concatenate([keep[...].astype(jnp.float32)] * windows, axis=1)
     size = F // BANDS
 
     def whiten(real, imag, gain):
@@ -256,6 +295,8 @@
                 cross[1, at, lanes] = (value - high.astype(jnp.float32)).astype(jnp.bfloat16)
 
     scale = 1.0 / math.sqrt(windows * F)
+    for read in reads:
+        read.wait()
     total = jnp.dot(inv_high[...], cross[0], preferred_element_type=jnp.float32)
     total += jnp.dot(inv_high[...], cross[1], preferred_element_type=jnp.float32)
     total += jnp.dot(inv_low[...], cross[0], preferred_element_type=jnp.float32)
@@ -268,43 +309,48 @@
     windows = tms * cores
     samples, channels = raw_records.shape[1:]
     count, reach, used, rows = layout(samples)
-    ids = source_ids.reshape(NSRC, 1)
-    keep = good_channels.astype(jnp.float32).reshape(1, LANES)
-    taps = jnp.tile(filter_taps.reshape(TAPS // 4, 4), (1, 96))
+    keep = good_channels.reshape(1, LANES)
     vmem = pl.BlockSpec(memory_space=pltpu.VMEM)
     smem = pl.BlockSpec(memory_space=pltpu.SMEM)
+    hbm = pl.BlockSpec(memory_space=pltpu.HBM)
     copies = chans - 1 + chans * (tms - 1 + cores - 1 + (tms - 1) * (cores - 1))
     gathered = pl.pallas_call(
         functools.partial(gather_kernel, sizes),
         out_shape=jax.ShapeDtypeStruct((windows, chans, rows + 16, LANES), jnp.bfloat16),
-        in_specs=[smem, vmem, vmem, vmem, vmem],
+        in_specs=[smem, smem, smem, vmem, hbm],
         out_specs=vmem,
         scratch_shapes=[
+            pltpu.VMEM((samples, channels), jnp.bfloat16),
             pltpu.VMEM((2, rows, 4 * rows + 256), jnp.bfloat16),
             pltpu.VMEM((chans, rows + 16, LANES), jnp.bfloat16),
+            pltpu.SemaphoreType.DMA,
             pltpu.SemaphoreType.DMA,
             pltpu.SemaphoreType.DMA((copies,)),
             pltpu.SemaphoreType.DMA((windows * chans,)),
         ],
         compiler_params=pltpu.CompilerParams(
-            collective_id=0, has_side_effects=True, vmem_limit_bytes=VMEM_LIMIT
+            collective_id=0, has_side_effects=True, vmem_limit_bytes=GATHER_VMEM
         ),
         name="gather",
-    )(window_offsets, taps, ids, keep, raw_records.reshape(samples, channels))
+    )(window_offsets, filter_taps, source_ids, keep, raw_records.reshape(samples, channels))
     mine = NSRC // windows
     return pl.pallas_call(
         functools.partial(correlate_kernel, sizes, samples),
         out_shape=jax.ShapeDtypeStruct((mine, LAGS, LANES), jnp.float32),
-        in_specs=[vmem] * 6,
+        in_specs=[smem, vmem, hbm, hbm, hbm, vmem],
         out_specs=vmem,
         scratch_shapes=[
             pltpu.VMEM((2 * F, windows * LANES), jnp.float32),
             pltpu.VMEM((2 * F, windows * NSRC), jnp.float32),
             pltpu.VMEM((2, 2 * F, mine * LANES), jnp.bfloat16),
+            pltpu.VMEM((4, F // 2, table.shape[1]), jnp.bfloat16),
+            pltpu.VMEM((LAGS, 2 * F), jnp.bfloat16),
+            pltpu.VMEM((LAGS, 2 * F), jnp.bfloat16),
+            pltpu.SemaphoreType.DMA((6,)),
         ],
-        compiler_params=pltpu.CompilerParams(vmem_limit_bytes=VMEM_LIMIT),
+        compiler_params=pltpu.CompilerParams(vmem_limit_bytes=CORRELATE_VMEM),
         name="correlate",
-    )(ids, keep, table, inv_high, inv_low, gathered)
+    )(source_ids, keep, table, inv_high, inv_low, gathered)
 
 
 def solution(mesh):

time: 35.8 us -> 36.8 us (1.028)
  Pallas kernels: 28.6 us -> 32.6 us
  local copies, waits for them, and re-layouts: 5.23 us -> 3.25 us
  other arithmetic: 0.81 us -> 0 us
    pallas_call x1, Pallas kernels: 8.45 us -> 11.5 us  [body(): pl.pallas_call(functools.partial(correlate_kernel, sizes, samples), out_s...]
    pallas_call x1, Pallas kernels: 20.2 us -> 21.1 us  [body(): pl.pallas_call(functools.partial(gather_kernel, sizes), out_shape=jax.Sha...]
    another operation x4 -> x0, local copies, waits for them, and re-layouts: 0.94 us -> none  [body(): taps = jnp.tile(filter_taps.reshape(TAPS // 4, 4), (1, 96))]
    reshape x1 -> x0, other arithmetic: 0.81 us -> none  [body(): keep = good_channels.astype(jnp.float32).reshape(1, LANES)]
    reshape x1 -> x0, local copies, waits for them, and re-layouts: 0.76 us -> none  [body(): ids = source_ids.reshape(NSRC, 1)]
    unnamed x8 -> x16, local copies, waits for them, and re-layouts: 3.54 us -> 3.25 us
where the time goes in v1:
time: 36.8 us; the launch traced here: 36.6 us
  Pallas kernels  32.6 us (89%)
  local copies, waits for them, and re-layouts  3.25 us (9%)
  between operations  0.73 us (2%)
    pallas_call x1, Pallas kernels, body(): pl.pallas_call(functools.partial(gather_kernel, sizes), out_shape=jax.Sha...  21.1 us
    pallas_call x1, Pallas kernels, body(): pl.pallas_call(functools.partial(correlate_kernel, sizes, samples), out_s...  11.5 us
    unnamed x16, local copies, waits for them, and re-layouts  3.25 us

profile of v1, /device:TPU:0, one launch (start us, length us, event | category | flops | bytes accessed | tf_op | source)
XLA Modules:
  0.0 36.6 jit_solution(5109174736156031637)
XLA Ops:
  0.0 0.0 copy-start.4
  0.0 0.0 copy-start.6
  0.7 0.0 copy-start
  0.7 1.2 %copy-done = bf16[1,1088,512]{2,1,0:T(8,128)(2,1)S(1)} copy-done((bf16[1,1088,512]{2,1,0:T(8,128)(2,1)S(1)}, bf16[1,1088,512]{2,1,0:T(8,128)(2,1)}, u32[]{:S(2)}) %copy-start) | copy-done | bytes 1114136
  1.9 0.0 copy-start.3
  1.9 0.7 %copy-done.3 = s32[4,4]{1,0:T(4,128)S(1)} copy-done((s32[4,4]{1,0:T(4,128)S(1)}, s32[4,4]{1,0:T(4,128)}, u32[]{:S(2)}) %copy-start.3) | copy-done | bytes 88
  2.6 0.0 copy-start.5
  2.6 0.7 %copy-done.5 = s32[128]{0:T(128)S(1)} copy-done((s32[128]{0:T(128)S(1)}, s32[128]{0:T(128)}, u32[]{:S(2)}) %copy-start.5) | copy-done | bytes 536
  3.3 0.0 copy-start.7
  3.3 0.7 %copy-done.7 = f32[64]{0:T(128)S(1)} copy-done((f32[64]{0:T(128)S(1)}, f32[64]{0:T(128)}, u32[]{:S(2)}) %copy-start.7) | copy-done | bytes 280
  3.9 0.0 copy-start.1
  3.9 0.0 copy-start.2
  3.9 21.1 %gather.1.blocks = bf16[4,4,400,128]{3,2,1,0:T(8,128)(2,1)S(1)} custom-call(s32[1]{0:T(128)S(6)} %copy.9.offset, f32[64]{0:T(128)S(1)} %copy-done.7, s32[4,4]{1,0:T(4,128)S(1)} %copy-done.3, s32[1,128]{1,0:T(1,128)S(1)} %bitcast.3, bf16[1088,512]{1,0:T(8,128)(2,1)S(1)} %bitcast.2), custom_call_target="tpu_custom_call" | custom-call | tf_op jit(solution)/shard_map/gather/pallas_call | solution.py:317
  25.1 0.0 copy-done.4
  25.1 0.0 copy-done.6
  25.1 0.0 copy-done.1
  25.1 0.0 copy-done.2
  25.1 11.5 %correlate.1 = f32[4,384,128]{2,1,0:T(8,128)} custom-call(s32[4,4]{1,0:T(4,128)S(1)} %copy-done.4, s32[1,128]{1,0:T(1,128)S(1)} %bitcast.4, bf16[1024,1536]{1,0:T(8,128)(2,1)} %constant.6.clone.table_hbm, bf16[384,1024]{1,0:T(8,128)(2,1)S(1)} %copy-done.2, bf16[384,1024]{1,0:T(8,128)(2,1)S(1)} %copy-done.1, bf16[4,4,400,128]{3,2,1,0:T(8,128)(2,1)S(1)} %gather.1.blocks), custom_call_target="tpu_custom_call" | custom-call | tf_op jit(solution)/shard_map/correlate/pallas_call | solution.py:337
Async XLA Ops:
  0.0 25.1 %copy-start.4 = (s32[4,4]{1,0:T(4,128)S(1)}, s32[4,4]{1,0:T(4,128)}, u32[]{:S(2)}) copy-start(s32[4,4]{1,0:T(4,128)} %ids.3) | copy-start | bytes 196
  0.0 25.1 %copy-start.6 = (s32[128]{0:T(128)S(1)}, s32[128]{0:T(128)}, u32[]{:S(2)}) copy-start(s32[128]{0:T(128)} %param.10) | copy-start | bytes 1540
  0.7 1.2 %copy-start = (bf16[1,1088,512]{2,1,0:T(8,128)(2,1)S(1)}, bf16[1,1088,512]{2,1,0:T(8,128)(2,1)}, u32[]{:S(2)}) copy-start(bf16[1,1088,512]{2,1,0:T(8,128)(2,1)} %param.8) | copy-start | bytes 3342340
  1.9 0.7 %copy-start.3 = (s32[4,4]{1,0:T(4,128)S(1)}, s32[4,4]{1,0:T(4,128)}, u32[]{:S(2)}) copy-start(s32[4,4]{1,0:T(4,128)} %ids.3) | copy-start | bytes 196
  2.6 0.7 %copy-start.5 = (s32[128]{0:T(128)S(1)}, s32[128]{0:T(128)}, u32[]{:S(2)}) copy-start(s32[128]{0:T(128)} %param.10) | copy-start | bytes 1540
  3.3 0.7 %copy-start.7 = (f32[64]{0:T(128)S(1)}, f32[64]{0:T(128)}, u32[]{:S(2)}) copy-start(f32[64]{0:T(128)} %taps.1) | copy-start | bytes 772
  3.9 21.2 %copy-start.1 = (bf16[384,1024]{1,0:T(8,128)(2,1)S(1)}, bf16[384,1024]{1,0:T(8,128)(2,1)}, u32[]{:S(2)}) copy-start(bf16[384,1024]{1,0:T(8,128)(2,1)} %constant.8.clone.low_hbm) | copy-start | bytes 2359300
  3.9 21.2 %copy-start.2 = (bf16[384,1024]{1,0:T(8,128)(2,1)S(1)}, bf16[384,1024]{1,0:T(8,128)(2,1)}, u32[]{:S(2)}) copy-start(bf16[384,1024]{1,0:T(8,128)(2,1)} %constant.7.clone.high_hbm) | copy-start | bytes 2359300

commit v2 on v0

--- a/solution.py
+++ b/solution.py
@@ -28,7 +28,7 @@
 
 def layout(samples):
     count = samples // 4
-    reach = TAPS // 4 - 1 + MAX_SHIFT
+    reach = TAPS // 4 + MAX_SHIFT
     used = up(count + reach, 16)
     rows = up(used, LANES)
     if used + rows // LANES * NSRC > rows:
@@ -41,25 +41,17 @@
     return np.concatenate([np.cos(angle), -np.sin(angle)], axis=0)
 
 
-def forward_blocks(chans, samples):
-    count, reach, used, rows = layout(samples)
+def forward_rows():
     freq = np.arange(1, F + 1, dtype=np.int64)[:, None]
-    parts = []
-    for owner in range(chans):
-        row = np.arange(rows, dtype=np.int64)
-        sample = count * owner - reach + row
-        inside = (sample >= 0) & (sample < W) & (row < used)
-        parts.append(waves(freq * sample[None, :]) * inside[None, :])
-    return np.concatenate(parts, axis=1).astype(np.float32).astype(ml_dtypes.bfloat16)
+    table = waves(freq * np.arange(W, dtype=np.int64)[None, :])
+    return table.astype(np.float32).astype(ml_dtypes.bfloat16)
 
 
 def inverse_rows():
     freq = np.arange(1, F + 1, dtype=np.int64)[:, None]
     shift = np.arange(LAGS, dtype=np.int64)[None, :] - LAGS // 2
     table = waves(freq * shift).astype(np.float32).T
-    high = table.astype(ml_dtypes.bfloat16)
-    low = (table - high.astype(np.float32)).astype(ml_dtypes.bfloat16)
-    return np.ascontiguousarray(high), np.ascontiguousarray(low)
+    return np.ascontiguousarray(table.astype(ml_dtypes.bfloat16))
 
 
 def gather_kernel(sizes, offset, taps, ids, keep, raw, out, toep, blocks, own_sem, send_sem, recv_sem):
@@ -82,7 +74,7 @@
     toep[...] = jnp.zeros_like(toep)
     row = lax.broadcasted_iota(jnp.int32, (32, 384), 0)
     col = lax.broadcasted_iota(jnp.int32, (32, 384), 1)
-    tap_group = (col >> 2) - row - 1 - (offset[0] >> 2)
+    tap_group = (col >> 2) - row - (offset[0] >> 2)
     base = jnp.zeros((32, 384), jnp.float32)
     for group in range(TAPS // 4):
         base = jnp.where(tap_group == group, taps[group : group + 1, :], base)
@@ -92,7 +84,7 @@
         span = slice(128 * block, 128 * block + 384)
         toep[0, 32 * block : 32 * block + 32, span] = high
         toep[1, 32 * block : 32 * block + 32, span] = low
-    lead = 4 * (reach + 1)
+    lead = 4 * reach
     samples_in = raw[...]
     total = jnp.dot(toep[0, :, lead : lead + samples], samples_in, preferred_element_type=jnp.float32)
     total += jnp.dot(toep[1, :, lead : lead + samples], samples_in, preferred_element_type=jnp.float32)
@@ -150,14 +142,16 @@
         send(blocks.at[there], window, here, {"chan": there})
     own = pltpu.make_async_copy(blocks.at[here], slot(window, here), own_sem)
     own.start()
-    own.wait()
     for step in range(chans):
         owner = lax.rem(here + chans - step, chans)
         if step:
             arrive(window, owner)
+        source = slot(window, owner) if step else blocks.at[here]
         for hop in range(1, tms):
-            send(slot(window, owner), window, owner, {"tm": lax.rem(tm + hop, tms)})
-        to_cores(window, owner)
+            send(source, window, owner, {"tm": lax.rem(tm + hop, tms)})
+        for turn in range(1, cores):
+            send(source, window, owner, {"src": lax.rem(core + turn, cores)})
+    own.wait()
     for step in range(chans):
         owner = lax.rem(here + chans - step, chans)
         for hop in range(1, tms):
@@ -174,40 +168,38 @@
         copy.wait_send()
 
 
-def correlate_kernel(sizes, samples, ids, keep, table, inv_high, inv_low, blocks, out, spec, src_spec, cross):
+def correlate_kernel(sizes, samples, ids, keep, table, inverse, blocks, out, spec, src_spec, cross, joined, src_joined):
     chans, tms, cores = sizes
     windows = tms * cores
-    _, _, used, rows = layout(samples)
+    count, reach, used, rows = layout(samples)
     mine = NSRC // windows
     window = lax.axis_index("tm") * cores + lax.axis_index("src")
     width = 2 if windows % 2 == 0 else 1
+    tiles = rows // LANES
+    joined[...] = jnp.zeros_like(joined)
+    src_joined[...] = jnp.zeros_like(src_joined)
+    for owner in range(chans):
+        at = slice(count * owner, count * owner + used)
+        for part in range(windows):
+            lanes = slice(part * LANES, (part + 1) * LANES)
+            joined[at, lanes] += blocks[part, owner, :used, :].astype(jnp.float32)
+        series = jnp.concatenate(
+            [
+                jnp.concatenate(
+                    [blocks[part, owner, used + NSRC * tile : used + NSRC * (tile + 1), :] for tile in range(tiles)],
+                    axis=1,
+                )
+                for part in range(windows)
+            ],
+            axis=0,
+        ).astype(jnp.float32)
+        src_joined[at, :] += series.T[:used, :]
     for first in range(0, windows, width):
-        data = jnp.concatenate(
-            [
-                jnp.concatenate([blocks[part, owner, :rows, :] for owner in range(chans)], axis=0)
-                for part in range(first, first + width)
-            ],
-            axis=1,
-        )
-        spec[:, first * LANES : (first + width) * LANES] = jnp.dot(
-            table[...], data, preferred_element_type=jnp.float32
-        )
-    tiles = rows // LANES
-    series = jnp.concatenate(
-        [
-            jnp.concatenate(
-                [
-                    blocks[part, owner, used + NSRC * tile : used + NSRC * (tile + 1), :]
-                    for owner in range(chans)
-                    for tile in range(tiles)
-                ],
-                axis=1,
-            )
-            for part in range(windows)
-        ],
-        axis=0,
-    )
-    src_spec[...] = lax.dot_general(table[...], series, NT, preferred_element_type=jnp.float32)
+        lanes = slice(first * LANES, (first + width) * LANES)
+        data = joined[reach : reach + W, lanes].astype(jnp.bfloat16)
+        spec[:, lanes] = jnp.dot(table[...], data, preferred_element_type=jnp.float32)
+    data = src_joined[reach : reach + W, :].astype(jnp.bfloat16)
+    src_spec[...] = jnp.dot(table[...], data, preferred_element_type=jnp.float32)
 
     channel = lax.broadcasted_iota(jnp.int32, (NSRC, LANES), 1)
     src_keep = jnp.zeros((NSRC, 1), jnp.float32)
@@ -256,14 +248,13 @@
                 cross[1, at, lanes] = (value - high.astype(jnp.float32)).astype(jnp.bfloat16)
 
     scale = 1.0 / math.sqrt(windows * F)
-    total = jnp.dot(inv_high[...], cross[0], preferred_element_type=jnp.float32)
-    total += jnp.dot(inv_high[...], cross[1], preferred_element_type=jnp.float32)
-    total += jnp.dot(inv_low[...], cross[0], preferred_element_type=jnp.float32)
+    total = jnp.dot(inverse[...], cross[0], preferred_element_type=jnp.float32)
+    total += jnp.dot(inverse[...], cross[1], preferred_element_type=jnp.float32)
     for one in range(mine):
         out[one] = total[:, one * LANES : (one + 1) * LANES] * scale
 
 
-def body(sizes, table, inv_high, inv_low, raw_records, filter_taps, good_channels, source_ids, window_offsets):
+def body(sizes, table, inverse, raw_records, filter_taps, good_channels, source_ids, window_offsets):
     chans, tms, cores = sizes
     windows = tms * cores
     samples, channels = raw_records.shape[1:]
@@ -295,16 +286,18 @@
     return pl.pallas_call(
         functools.partial(correlate_kernel, sizes, samples),
         out_shape=jax.ShapeDtypeStruct((mine, LAGS, LANES), jnp.float32),
-        in_specs=[vmem] * 6,
+        in_specs=[vmem] * 5,
         out_specs=vmem,
         scratch_shapes=[
             pltpu.VMEM((2 * F, windows * LANES), jnp.float32),
             pltpu.VMEM((2 * F, windows * NSRC), jnp.float32),
             pltpu.VMEM((2, 2 * F, mine * LANES), jnp.bfloat16),
+            pltpu.VMEM((up(count * (chans - 1) + used, 8), windows * LANES), jnp.float32),
+            pltpu.VMEM((up(count * (chans - 1) + used, 8), windows * NSRC), jnp.float32),
         ],
         compiler_params=pltpu.CompilerParams(vmem_limit_bytes=VMEM_LIMIT),
         name="correlate",
-    )(ids, keep, table, inv_high, inv_low, gathered)
+    )(ids, keep, table, inverse, gathered)
 
 
 def solution(mesh):
@@ -318,9 +311,7 @@
     sizes = tuple(mesh.shape[name] for name in ("chan", "tm", "src"))
 
     def run(raw_records, *rest):
-        table = forward_blocks(sizes[0], raw_records.shape[1])
-        inv_high, inv_low = inverse_rows()
-        return body(sizes, table, inv_high, inv_low, raw_records, *rest)
+        return body(sizes, forward_rows(), inverse_rows(), raw_records, *rest)
 
     def call(raw_records, *rest):
         return jax.shard_map(

time: 35.8 us -> 32.2 us (0.90)
  local copies, waits for them, and re-layouts: 5.23 us -> 2.97 us
  Pallas kernels: 28.6 us -> 27.6 us
    unnamed x8 -> x6, local copies, waits for them, and re-layouts: 3.54 us -> 1.28 us
    pallas_call x1, Pallas kernels: 8.45 us -> 7.37 us  [body(): pl.pallas_call(functools.partial(correlate_kernel, sizes, samples), out_s...]
where the time goes in v2:
time: 32.2 us; the launch traced here: 32 us
  Pallas kernels  27.6 us (86%)
  local copies, waits for them, and re-layouts  2.97 us (9%)
  between operations  0.84 us (3%)
  other arithmetic  0.66 us (2%)
    pallas_call x1, Pallas kernels, body(): pl.pallas_call(functools.partial(gather_kernel, sizes), out_shape=jax.Sha...  20.2 us
    pallas_call x1, Pallas kernels, body(): pl.pallas_call(functools.partial(correlate_kernel, sizes, samples), out_s...  7.37 us
    unnamed x6, local copies, waits for them, and re-layouts  1.28 us
    another operation x4, local copies, waits for them, and re-layouts, body(): taps = jnp.tile(filter_taps.reshape(TAPS // 4, 4), (1, 96))  0.94 us
    reshape x1, local copies, waits for them, and re-layouts, body(): ids = source_ids.reshape(NSRC, 1)  0.76 us
    reshape x1, other arithmetic, body(): keep = good_channels.astype(jnp.float32).reshape(1, LANES)  0.66 us

profile of v2, /device:TPU:0, one launch (start us, length us, event | category | flops | bytes accessed | tf_op | source)
XLA Modules:
  0.0 32.0 jit_solution(4885155494605855433)
XLA Ops:
  0.0 0.0 copy-start
  0.8 0.7 %convert_bitcast_fusion.keep = f32[1,128]{1,0:T(1,128)S(1)} fusion(s32[128]{0:T(128)} %param.9), kind=kLoop, calls=%fused_computation | loop fusion | flops 128 | bytes 1024 | tf_op jit(solution)/shard_map/reshape | solution.py:263
  1.5 0.8 %reshape.16.ids = s32[16,1]{1,0:T(8,128)S(1)} reshape(s32[4,4]{1,0:T(4,128)} %param.10) | data formatting | bytes 128 | tf_op jit(solution)/shard_map/reshape | solution.py:262
  2.2 0.7 %tile.10 = f32[16,4]{1,0:T(8,128)S(1)} reshape(f32[64]{0:T(128)} %param.8) | data formatting | bytes 512 | tf_op jit(solution)/shard_map/tile | solution.py:264
  3.0 0.1 copy.10
  3.1 0.1 copy.11.taps
  3.2 0.0 copy-start.1
  3.2 1.3 %copy-done.1 = bf16[1,1088,512]{2,1,0:T(8,128)(2,1)S(1)} copy-done((bf16[1,1088,512]{2,1,0:T(8,128)(2,1)S(1)}, bf16[1,1088,512]{2,1,0:T(8,128)(2,1)}, u32[]{:S(2)}) %copy-start.1) | copy-done | bytes 1114136
  4.4 0.0 copy-start.2
  4.4 20.2 %gather.1.blocks = bf16[4,4,400,128]{3,2,1,0:T(8,128)(2,1)S(1)} custom-call(s32[1]{0:T(128)S(6)} %copy.14.offset, f32[16,384]{1,0:T(8,128)S(1)} %copy.11.taps, s32[16,1]{1,0:T(8,128)S(1)} %reshape.16.ids, f32[1,128]{1,0:T(1,128)S(1)} %convert_bitcast_fusion.keep, bf16[1088,512]{1,0:T(8,128)(2,1)S(1)} %bitcast.4), custom_call_target="tpu_custom_call" | custom-call | tf_op jit(solution)/shard_map/gather/pallas_call | solution.py:268
  24.6 0.0 copy-done
  24.6 0.0 copy-done.2
  24.7 7.4 %correlate.1 = f32[4,384,128]{2,1,0:T(8,128)} custom-call(s32[16,1]{1,0:T(8,128)S(1)} %reshape.16.ids, f32[1,128]{1,0:T(1,128)S(1)} %convert_bitcast_fusion.keep, bf16[1024,1024]{1,0:T(8,128)(2,1)S(1)} %copy-done, bf16[384,1024]{1,0:T(8,128)(2,1)S(1)} %copy-done.2, bf16[4,4,400,128]{3,2,1,0:T(8,128)(2,1)S(1)} %gather.1.blocks), custom_call_target="tpu_custom_call" | custom-call | tf_op jit(solution)/shard_map/correlate/pallas_call | solution.py:286
  (1 shorter events, 0.0 us)
Async XLA Ops:
  0.0 24.6 %copy-start = (bf16[1024,1024]{1,0:T(8,128)(2,1)S(1)}, bf16[1024,1024]{1,0:T(8,128)(2,1)}, u32[]{:S(2)}) copy-start(bf16[1024,1024]{1,0:T(8,128)(2,1)} %constant.4.clone.table) | copy-start | bytes 6291460
  3.2 1.3 %copy-start.1 = (bf16[1,1088,512]{2,1,0:T(8,128)(2,1)S(1)}, bf16[1,1088,512]{2,1,0:T(8,128)(2,1)}, u32[]{:S(2)}) copy-start(bf16[1,1088,512]{2,1,0:T(8,128)(2,1)} %param.7) | copy-start | bytes 3342340
  4.4 20.2 %copy-start.2 = (bf16[384,1024]{1,0:T(8,128)(2,1)S(1)}, bf16[384,1024]{1,0:T(8,128)(2,1)}, u32[]{:S(2)}) copy-start(bf16[384,1024]{1,0:T(8,128)(2,1)} %constant.5.clone.inverse) | copy-start | bytes 2359300

commit v3 on v2

--- a/solution.py
+++ b/solution.py
@@ -28,12 +28,10 @@
 
 def layout(samples):
     count = samples // 4
-    reach = TAPS // 4 + MAX_SHIFT
+    reach = TAPS // 4
     used = up(count + reach, 16)
     rows = up(used, LANES)
-    if used + rows // LANES * NSRC > rows:
-        rows = up(used + rows // LANES * NSRC, LANES)
-    return count, reach, used, rows
+    return count, reach, used, rows, used + rows // LANES * NSRC
 
 
 def waves(phase):
@@ -57,7 +55,7 @@
 def gather_kernel(sizes, offset, taps, ids, keep, raw, out, toep, blocks, own_sem, send_sem, recv_sem):
     chans, tms, cores = sizes
     samples, channels = raw.shape
-    count, reach, used, rows = layout(samples)
+    count, reach, used, rows, flag_row = layout(samples)
     here, tm, core = (lax.axis_index(name) for name in ("chan", "tm", "src"))
     window = tm * cores + core
 
@@ -74,7 +72,7 @@
     toep[...] = jnp.zeros_like(toep)
     row = lax.broadcasted_iota(jnp.int32, (32, 384), 0)
     col = lax.broadcasted_iota(jnp.int32, (32, 384), 1)
-    tap_group = (col >> 2) - row - (offset[0] >> 2)
+    tap_group = (col >> 2) - row - (LANES // 4 - reach)
     base = jnp.zeros((32, 384), jnp.float32)
     for group in range(TAPS // 4):
         base = jnp.where(tap_group == group, taps[group : group + 1, :], base)
@@ -84,7 +82,7 @@
         span = slice(128 * block, 128 * block + 384)
         toep[0, 32 * block : 32 * block + 32, span] = high
         toep[1, 32 * block : 32 * block + 32, span] = low
-    lead = 4 * reach
+    lead = LANES
     samples_in = raw[...]
     total = jnp.dot(toep[0, :, lead : lead + samples], samples_in, preferred_element_type=jnp.float32)
     total += jnp.dot(toep[1, :, lead : lead + samples], samples_in, preferred_element_type=jnp.float32)
@@ -92,17 +90,14 @@
     channel = lax.broadcasted_iota(jnp.int32, (NSRC, channels), 1)
     pick = jnp.where(channel == ids[...], 1.0, 0.0).astype(jnp.bfloat16)
     picked = lax.dot_general(pick, filtered, NT, preferred_element_type=jnp.float32).astype(jnp.bfloat16)
-    keep_rows = jnp.broadcast_to(keep[...], (16, LANES)).astype(jnp.bfloat16)
+    shift = jnp.full((8, LANES), offset[0] >> 2, jnp.int32).astype(jnp.float32)
+    keep_rows = jnp.concatenate([jnp.broadcast_to(keep[...], (8, LANES)), shift], axis=0).astype(jnp.bfloat16)
     for owner in range(chans):
         blocks[owner, :used, :] = filtered[:used, owner * LANES : (owner + 1) * LANES]
-        for tile in range((rows - used) // NSRC):
+        for tile in range(rows // LANES):
             at = used + tile * NSRC
-            lanes = slice(tile * LANES, (tile + 1) * LANES)
-            if tile < rows // LANES:
-                blocks[owner, at : at + NSRC, :] = picked[:, lanes]
-            else:
-                blocks[owner, at : at + NSRC, :] = jnp.zeros((NSRC, LANES), jnp.bfloat16)
-        blocks[owner, rows:, :] = keep_rows
+            blocks[owner, at : at + NSRC, :] = picked[:, tile * LANES : (tile + 1) * LANES]
+        blocks[owner, flag_row:, :] = keep_rows
 
     pl.semaphore_wait(barrier, chans + tms + cores - 3)
 
@@ -171,7 +166,7 @@
 def correlate_kernel(sizes, samples, ids, keep, table, inverse, blocks, out, spec, src_spec, cross, joined, src_joined):
     chans, tms, cores = sizes
     windows = tms * cores
-    count, reach, used, rows = layout(samples)
+    count, reach, used, rows, flag_row = layout(samples)
     mine = NSRC // windows
     window = lax.axis_index("tm") * cores + lax.axis_index("src")
     width = 2 if windows % 2 == 0 else 1
@@ -181,8 +176,7 @@
     for owner in range(chans):
         at = slice(count * owner, count * owner + used)
         for part in range(windows):
-            lanes = slice(part * LANES, (part + 1) * LANES)
-            joined[at, lanes] += blocks[part, owner, :used, :].astype(jnp.float32)
+            joined[part, at, :] += blocks[part, owner, :used, :].astype(jnp.float32)
         series = jnp.concatenate(
             [
                 jnp.concatenate(
@@ -193,18 +187,32 @@
             ],
             axis=0,
         ).astype(jnp.float32)
-        src_joined[at, :] += series.T[:used, :]
+        src_joined[at, : windows * NSRC] += series.T[:used, :]
+    starts = [
+        jnp.max(blocks[part, 0, flag_row : flag_row + 16, :].astype(jnp.float32)[8:]).astype(jnp.int32) + reach
+        for part in range(windows)
+    ]
     for first in range(0, windows, width):
         lanes = slice(first * LANES, (first + width) * LANES)
-        data = joined[reach : reach + W, lanes].astype(jnp.bfloat16)
+        data = jnp.concatenate(
+            [
+                joined[part, pl.ds(starts[part], W), :].astype(jnp.bfloat16)
+                for part in range(first, first + width)
+            ],
+            axis=1,
+        )
         spec[:, lanes] = jnp.dot(table[...], data, preferred_element_type=jnp.float32)
-    data = src_joined[reach : reach + W, :].astype(jnp.bfloat16)
+    part_at = lax.broadcasted_iota(jnp.int32, (W, windows * NSRC), 1) // NSRC
+    data = jnp.zeros((W, windows * NSRC), jnp.float32)
+    for part in range(windows):
+        data = jnp.where(part_at == part, src_joined[pl.ds(starts[part], W), :][:, : windows * NSRC], data)
+    data = data.astype(jnp.bfloat16)
     src_spec[...] = jnp.dot(table[...], data, preferred_element_type=jnp.float32)
 
     channel = lax.broadcasted_iota(jnp.int32, (NSRC, LANES), 1)
     src_keep = jnp.zeros((NSRC, 1), jnp.float32)
     for owner in range(chans):
-        flags = blocks[0, owner, rows : rows + 16, :].astype(jnp.float32)
+        flags = blocks[0, owner, flag_row : flag_row + 16, :].astype(jnp.float32)[:1]
         hit = channel + owner * LANES == ids[...]
         src_keep += jnp.sum(jnp.where(hit, flags, 0.0), axis=1, keepdims=True)
     number = lax.broadcasted_iota(jnp.int32, (NSRC, mine * LANES), 0)
@@ -258,7 +266,7 @@
     chans, tms, cores = sizes
     windows = tms * cores
     samples, channels = raw_records.shape[1:]
-    count, reach, used, rows = layout(samples)
+    count, reach, used, rows, flag_row = layout(samples)
     ids = source_ids.reshape(NSRC, 1)
     keep = good_channels.astype(jnp.float32).reshape(1, LANES)
     taps = jnp.tile(filter_taps.reshape(TAPS // 4, 4), (1, 96))
@@ -267,18 +275,23 @@
     copies = chans - 1 + chans * (tms - 1 + cores - 1 + (tms - 1) * (cores - 1))
     gathered = pl.pallas_call(
         functools.partial(gather_kernel, sizes),
-        out_shape=jax.ShapeDtypeStruct((windows, chans, rows + 16, LANES), jnp.bfloat16),
+        out_shape=jax.ShapeDtypeStruct((windows, chans, flag_row + 16, LANES), jnp.bfloat16),
         in_specs=[smem, vmem, vmem, vmem, vmem],
         out_specs=vmem,
         scratch_shapes=[
             pltpu.VMEM((2, rows, 4 * rows + 256), jnp.bfloat16),
-            pltpu.VMEM((chans, rows + 16, LANES), jnp.bfloat16),
+            pltpu.VMEM((chans, flag_row + 16, LANES), jnp.bfloat16),
             pltpu.SemaphoreType.DMA,
             pltpu.SemaphoreType.DMA((copies,)),
             pltpu.SemaphoreType.DMA((windows * chans,)),
         ],
         compiler_params=pltpu.CompilerParams(
             collective_id=0, has_side_effects=True, vmem_limit_bytes=VMEM_LIMIT
+        ),
+        cost_estimate=pl.CostEstimate(
+            flops=4 * rows * samples * channels,
+            bytes_accessed=2 * samples * channels + 2 * (copies + windows * chans) * (flag_row + 16) * LANES,
+            transcendentals=0,
         ),
         name="gather",
     )(window_offsets, taps, ids, keep, raw_records.reshape(samples, channels))
@@ -292,8 +305,8 @@
             pltpu.VMEM((2 * F, windows * LANES), jnp.float32),
             pltpu.VMEM((2 * F, windows * NSRC), jnp.float32),
             pltpu.VMEM((2, 2 * F, mine * LANES), jnp.bfloat16),
-            pltpu.VMEM((up(count * (chans - 1) + used, 8), windows * LANES), jnp.float32),
-            pltpu.VMEM((up(count * (chans - 1) + used, 8), windows * NSRC), jnp.float32),
+            pltpu.VMEM((windows, up(count * (chans - 1) + used, 8), LANES), jnp.float32),
+            pltpu.VMEM((up(count * (chans - 1) + used, 8), LANES), jnp.float32),
         ],
         compiler_params=pltpu.CompilerParams(vmem_limit_bytes=VMEM_LIMIT),
         name="correlate",

time: 32.2 us -> 31.3 us (0.972)
  Pallas kernels: 27.6 us -> 26.7 us
    pallas_call x1, Pallas kernels: 20.2 us -> 19.2 us  [body(): pl.pallas_call(functools.partial(gather_kernel, sizes), out_shape=jax.Sha...]
where the time goes in v3:
time: 31.3 us; the launch traced here: 31.1 us
  Pallas kernels  26.7 us (85%)
  local copies, waits for them, and re-layouts  2.97 us (9%)
  between operations  0.69 us (2%)
  other arithmetic  0.66 us (2%)
    pallas_call x1, Pallas kernels, body(): pl.pallas_call(functools.partial(gather_kernel, sizes), out_shape=jax.Sha...  19.2 us
    pallas_call x1, Pallas kernels, body(): pl.pallas_call(functools.partial(correlate_kernel, sizes, samples), out_s...  7.58 us
    unnamed x6, local copies, waits for them, and re-layouts  1.28 us
    another operation x4, local copies, waits for them, and re-layouts, body(): taps = jnp.tile(filter_taps.reshape(TAPS // 4, 4), (1, 96))  0.94 us
    reshape x1, local copies, waits for them, and re-layouts, body(): ids = source_ids.reshape(NSRC, 1)  0.76 us
    reshape x1, other arithmetic, body(): keep = good_channels.astype(jnp.float32).reshape(1, LANES)  0.66 us

profile of v3, /device:TPU:0, one launch (start us, length us, event | category | flops | bytes accessed | tf_op | source)
XLA Modules:
  0.0 31.1 jit_solution(2682820895203280210)
XLA Ops:
  0.7 0.7 %convert_bitcast_fusion.keep = f32[1,128]{1,0:T(1,128)S(1)} fusion(s32[128]{0:T(128)} %param.9), kind=kLoop, calls=%fused_computation | loop fusion | flops 128 | bytes 1024 | tf_op jit(solution)/shard_map/reshape | solution.py:271
  1.3 0.8 %reshape.16.ids = s32[16,1]{1,0:T(8,128)S(1)} reshape(s32[4,4]{1,0:T(4,128)} %param.10) | data formatting | bytes 128 | tf_op jit(solution)/shard_map/reshape | solution.py:270
  2.1 0.7 %tile.10 = f32[16,4]{1,0:T(8,128)S(1)} reshape(f32[64]{0:T(128)} %param.8) | data formatting | bytes 512 | tf_op jit(solution)/shard_map/tile | solution.py:272
  2.8 0.1 copy.10
  2.9 0.1 copy.11.taps
  3.0 0.0 copy-start.2
  3.0 1.3 %copy-done.2 = bf16[1,1088,512]{2,1,0:T(8,128)(2,1)S(1)} copy-done((bf16[1,1088,512]{2,1,0:T(8,128)(2,1)S(1)}, bf16[1,1088,512]{2,1,0:T(8,128)(2,1)}, u32[]{:S(2)}) %copy-start.2) | copy-done | bytes 1114136
  4.3 0.0 copy-start
  4.3 0.0 copy-start.1
  4.3 19.2 %gather.1.blocks = bf16[4,4,352,128]{3,2,1,0:T(8,128)(2,1)S(1)} custom-call(s32[1]{0:T(128)S(6)} %copy.14.offset, f32[16,384]{1,0:T(8,128)S(1)} %copy.11.taps, s32[16,1]{1,0:T(8,128)S(1)} %reshape.16.ids, f32[1,128]{1,0:T(1,128)S(1)} %convert_bitcast_fusion.keep, bf16[1088,512]{1,0:T(8,128)(2,1)S(1)} %bitcast.4), custom_call_target="tpu_custom_call" | custom-call | flops 855638016 | bytes 3907584 | tf_op jit(solution)/shard_map/gather/pallas_call | solution.py:276
  23.5 0.0 copy-done
  23.5 0.0 copy-done.1
  23.5 7.6 %correlate.1 = f32[4,384,128]{2,1,0:T(8,128)} custom-call(s32[16,1]{1,0:T(8,128)S(1)} %reshape.16.ids, f32[1,128]{1,0:T(1,128)S(1)} %convert_bitcast_fusion.keep, bf16[1024,1024]{1,0:T(8,128)(2,1)S(1)} %copy-done, bf16[384,1024]{1,0:T(8,128)(2,1)S(1)} %copy-done.1, bf16[4,4,352,128]{3,2,1,0:T(8,128)(2,1)S(1)} %gather.1.blocks), custom_call_target="tpu_custom_call" | custom-call | tf_op jit(solution)/shard_map/correlate/pallas_call | solution.py:299
  (1 shorter events, 0.0 us)
Async XLA Ops:
  3.0 1.3 %copy-start.2 = (bf16[1,1088,512]{2,1,0:T(8,128)(2,1)S(1)}, bf16[1,1088,512]{2,1,0:T(8,128)(2,1)}, u32[]{:S(2)}) copy-start(bf16[1,1088,512]{2,1,0:T(8,128)(2,1)} %param.7) | copy-start | bytes 3342340
  4.3 19.2 %copy-start = (bf16[1024,1024]{1,0:T(8,128)(2,1)S(1)}, bf16[1024,1024]{1,0:T(8,128)(2,1)}, u32[]{:S(2)}) copy-start(bf16[1024,1024]{1,0:T(8,128)(2,1)} %constant.4.clone.table) | copy-start | bytes 6291460
  4.3 19.2 %copy-start.1 = (bf16[384,1024]{1,0:T(8,128)(2,1)S(1)}, bf16[384,1024]{1,0:T(8,128)(2,1)}, u32[]{:S(2)}) copy-start(bf16[384,1024]{1,0:T(8,128)(2,1)} %constant.5.clone.inverse) | copy-start | bytes 2359300
